TPU v7x, 32 devices: a whole 2x2x4 slice. The times are simulated.
32 devices in a mesh: dp: 4 (over z), ctx: 8 (over y, x, core).
Axes of the slice: x: 2, y: 2, z: 4, core: 2. Of those that a mesh axis runs over, the one named last changes fastest.
Arguments:
- streams: bfloat16 [3, 1, 2560, 8192], P(None, None, 'ctx', 'dp'), may hold values from -6 to 6
- cotangent: bfloat16 [1, 2560, 8192], P(None, 'ctx', 'dp'), may hold values from -6 to 6
- counts: int32 [1, 8], P(None, 'ctx'), may hold values from 1 to 320, as said below
- short_filters: bfloat16 [3, 7, 8192], P(None, None, ('dp', 'ctx')), may hold values from -14 to 14
- long_filter: bfloat16 [128, 8192], P(None, ('dp', 'ctx')), may hold values from -0.5 to 0.5
Outputs:
- stream_grads: bfloat16 [3, 1, 2560, 8192], P(None, None, 'ctx', 'dp')
- long_grad: float32 [128, 8192], P(None, ('dp', 'ctx'))
- short_grad: float32 [3, 7, 8192], P(None, None, ('dp', 'ctx'))
Inputs may be any that keep to these rules, and one draw needn't show every extreme that they name: In each window the counts sum to 2048, and one of them equals 320.
All inputs are finite; a program needn't handle non-finite values.
Results may differ from a plain program's by a relative error of at most 0.0058.
Values may be sent and summed in bfloat16 or wider, within the bound.
A program may use at most 128 MiB of HBM per device.

v0:
```python
import jax
import jax.numpy as jnp
from jax import lax
from jax.sharding import PartitionSpec as P

CH = 8192
LTAP = 128
STAP = 7


def carried_in(value, axis, join, neutral, backward):
    count, mine = (lax.axis_size(axis), lax.axis_index(axis))
    pieces = jax.tree.map(lambda part: lax.all_gather(part, axis), value)
    if backward:
        pieces = jax.tree.map(lambda part: part[::-1], pieces)
        mine = count - 1 - mine
    running = jax.tree.map(
        lambda part, zero: jnp.full_like(part, 0) + jnp.asarray(zero, part.dtype), value, neutral
    )

    def hop(position, running):
        longer = join(running, jax.tree.map(lambda part: part[position], pieces))
        return jax.tree.map(lambda new, old: jnp.where(position < mine, new, old), longer, running)

    return lax.fori_loop(0, count - 1, hop, running)


def causal_long(lead, filt, length):
    reach = filt.shape[0] - 1

    def causal_add_tap(tap_index, total):
        piece = lax.dynamic_slice_in_dim(lead, reach - tap_index, length, 0)
        return total + filt[tap_index].astype(jnp.float32)[None, :] * piece.astype(jnp.float32)

    return lax.fori_loop(
        0, filt.shape[0], causal_add_tap, jnp.zeros((length, filt.shape[1]), jnp.float32)
    )


def anticausal_long(trail, filt, length):

    def anticausal_add_tap(tap_index, total):
        piece = lax.dynamic_slice_in_dim(trail, tap_index, length, 0)
        return total + filt[tap_index].astype(jnp.float32)[None, :] * piece.astype(jnp.float32)

    return lax.fori_loop(
        0, filt.shape[0], anticausal_add_tap, jnp.zeros((length, filt.shape[1]), jnp.float32)
    )


def tap_products(lead, grad_rows, taps):
    reach = taps - 1
    length = grad_rows.shape[0]

    def one_tap(tap_index):
        piece = lax.dynamic_slice_in_dim(lead, reach - tap_index, length, 0)
        return jnp.sum(grad_rows.astype(jnp.float32) * piece.astype(jnp.float32), axis=0)

    return lax.map(one_tap, jnp.arange(taps, dtype=jnp.int32))


def short_forward(leading, filters, length):
    taps = filters.shape[1]
    summed = jnp.zeros((filters.shape[0], length, filters.shape[2]), jnp.float32)
    for tap_index in range(taps):
        start = taps - 1 - tap_index
        summed = summed + filters[:, tap_index][:, None, :].astype(jnp.float32) * leading[
            :, start : start + length
        ].astype(jnp.float32)
    return summed


def short_backward(trailing, filters, length):
    taps = filters.shape[1]
    summed = jnp.zeros((filters.shape[0], length, filters.shape[2]), jnp.float32)
    for tap_index in range(taps):
        summed = summed + filters[:, tap_index][:, None, :].astype(jnp.float32) * trailing[
            :, tap_index : tap_index + length
        ].astype(jnp.float32)
    return summed


def last_rows(block, live_count, length):
    zero_rows = jnp.zeros(block.shape[:-2] + (length, block.shape[-1]), block.dtype)
    padded = jnp.concatenate([zero_rows, block], axis=-2)
    return lax.dynamic_slice_in_dim(padded, live_count, length, axis=block.ndim - 2)


def first_rows(block, length):
    zero_rows = jnp.zeros(block.shape[:-2] + (length, block.shape[-1]), block.dtype)
    padded = jnp.concatenate([block, zero_rows], axis=-2)
    return padded[..., :length, :]


def fill_of(live_count, length):
    return jnp.minimum(live_count, length).astype(jnp.bfloat16).reshape(1)


def join_fills(earlier, later):
    longest = max((member.shape[-2] for member in earlier[:-1]))
    summed = earlier[-1].astype(jnp.float32) + later[-1].astype(jnp.float32)
    return jnp.minimum(summed, float(longest)).astype(earlier[-1].dtype)


def join_tails(earlier, later):
    moved_by = later[-1][0].astype(jnp.int32)
    joined = []
    for before, after in zip(earlier[:-1], later[:-1]):
        length = before.shape[-2]
        extended = jnp.concatenate([before, jnp.zeros_like(before)], axis=-2)
        moved = lax.dynamic_slice_in_dim(extended, moved_by, length, axis=before.ndim - 2)
        row_ids = lax.broadcasted_iota(jnp.int32, (length, 1), 0)
        joined.append(jnp.where(row_ids >= length - moved_by, after, moved))
    return tuple(joined) + (join_fills(earlier, later),)


def join_heads(earlier, later):
    moved_by = later[-1][0].astype(jnp.int32)
    joined = []
    for further, nearer in zip(earlier[:-1], later[:-1]):
        length = further.shape[-2]
        extended = jnp.concatenate([jnp.zeros_like(further), further], axis=-2)
        moved = lax.dynamic_slice_in_dim(extended, length - moved_by, length, axis=further.ndim - 2)
        row_ids = lax.broadcasted_iota(jnp.int32, (length, 1), 0)
        joined.append(jnp.where(row_ids < moved_by, nearer, moved))
    return tuple(joined) + (join_fills(earlier, later),)


def local(streams, cotangent, counts, short_filters, long_filter):
    live_count = counts[0, 0]
    slot_count = streams.shape[2]
    channels = streams.shape[3]
    reach = LTAP - 1
    short_reach = STAP - 1
    zero_fill = jnp.zeros((1,), jnp.bfloat16)
    live = lax.broadcasted_iota(jnp.int32, (slot_count, 1), 0) < live_count
    source = jnp.where(live[None], streams[:, 0], jnp.zeros((), streams.dtype))
    grad_out = jnp.where(live, cotangent[0], jnp.zeros((), cotangent.dtype))
    long_full, short_full = (
        lax.all_gather(long_filter, "ctx", axis=1, tiled=True),
        lax.all_gather(short_filters, "ctx", axis=2, tiled=True),
    )
    query_tail = last_rows(source[0:1], live_count, short_reach)
    pair_tail = last_rows(source[1:3], live_count, reach + short_reach)
    query_halo, pair_halo, _ = carried_in(
        (query_tail, pair_tail, fill_of(live_count, reach + short_reach)),
        "ctx",
        join_tails,
        (jnp.zeros_like(query_tail), jnp.zeros_like(pair_tail), zero_fill),
        False,
    )
    leading = jnp.concatenate(
        [jnp.concatenate([query_halo, pair_halo[:, reach:]], axis=0), source], axis=1
    )
    query = short_forward(
        jnp.concatenate([query_halo, source[0:1]], axis=1), short_full[0:1], slot_count
    )[0]
    pair_lead = jnp.concatenate([pair_halo, source[1:3]], axis=1)
    pair_feats = short_forward(pair_lead, short_full[1:3], reach + slot_count)
    keep_rows = lax.broadcasted_iota(jnp.int32, (reach + slot_count, 1), 0) < reach + live_count
    gated_lead = jnp.where(keep_rows, pair_feats[0] * pair_feats[1], 0.0).astype(jnp.bfloat16)
    keys = pair_feats[0, reach:]
    values = pair_feats[1, reach:]
    long_out = causal_long(gated_lead, long_full, slot_count)
    grad_query = (grad_out * long_out).astype(jnp.bfloat16)
    grad_long = (grad_out * query).astype(jnp.bfloat16)
    long_head = first_rows(grad_long, reach)
    long_halo, _ = carried_in(
        (long_head, fill_of(live_count, reach)),
        "ctx",
        join_heads,
        (jnp.zeros_like(long_head), zero_fill),
        True,
    )
    trailing = jnp.concatenate([grad_long, jnp.zeros((reach, channels), jnp.bfloat16)], axis=0)
    trailing = lax.dynamic_update_slice_in_dim(trailing, long_halo, live_count, 0)
    grad_gated = anticausal_long(trailing, long_full, slot_count)
    grad_keys = jnp.where(live, grad_gated * values, 0.0).astype(jnp.bfloat16)
    grad_values = jnp.where(live, grad_gated * keys, 0.0).astype(jnp.bfloat16)
    grads = jnp.stack([grad_query, grad_keys, grad_values])
    grad_head = first_rows(grads, short_reach)
    grad_halo, _ = carried_in(
        (grad_head, fill_of(live_count, short_reach)),
        "ctx",
        join_heads,
        (jnp.zeros_like(grad_head), zero_fill),
        True,
    )
    grad_trail = jnp.concatenate(
        [grads, jnp.zeros((3, short_reach, channels), jnp.bfloat16)], axis=1
    )
    grad_trail = lax.dynamic_update_slice_in_dim(grad_trail, grad_halo, live_count, 1)
    back = short_backward(grad_trail, short_full, slot_count)
    stream_grads = jnp.where(live[None], back, 0.0).astype(jnp.bfloat16)[:, None]
    long_term = tap_products(gated_lead, grad_long, LTAP)
    short_terms = []
    for tap_index in range(STAP):
        start = short_reach - tap_index
        short_terms.append(
            jnp.sum(
                grads.astype(jnp.float32)
                * leading[:, start : start + slot_count].astype(jnp.float32),
                axis=1,
            )
        )
    short_term = jnp.stack(short_terms, axis=1)
    grad_rows = jnp.concatenate([long_term, short_term.reshape(3 * STAP, channels)], axis=0)
    summed = lax.psum(grad_rows, "ctx")
    squares = lax.psum(jnp.sum(summed * summed), "dp")
    share_width = channels // lax.axis_size("ctx")
    own_share = lax.dynamic_slice_in_dim(
        summed, lax.axis_index("ctx") * share_width, share_width, 1
    )
    rms = jnp.sqrt(squares / float((LTAP + 3 * STAP) * CH) + 1e-06)
    normed = own_share / rms
    long_grad = normed[:LTAP]
    short_grad = normed[LTAP:].reshape(3, STAP, normed.shape[1])
    return (stream_grads, long_grad, short_grad)


def solution(mesh):
    return jax.shard_map(
        local,
        mesh=mesh,
        in_specs=(
            P(None, None, "ctx", "dp"),
            P(None, "ctx", "dp"),
            P(None, "ctx"),
            P(None, None, ("dp", "ctx")),
            P(None, ("dp", "ctx")),
        ),
        out_specs=(
            P(None, None, "ctx", "dp"),
            P(None, ("dp", "ctx")),
            P(None, None, ("dp", "ctx")),
        ),
        check_vma=False,
    )
```

profile of v0, /device:TPU:0, one launch (start us, length us, event | category | flops | bytes accessed | tf_op | source)
XLA Modules:
  0.0 1718.8 jit_solution(17610833392057801315)
XLA Ops:
  17.2 15.3 all-reduce.11
  35.1 8.4 all_gather.39
  45.8 10.4 all-gather
  56.3 15.5 all_gather.40
  72.6 5.0 all-gather.8.cloned.1.call-done
  77.6 26.1 %while.91 = (s32[]{:T(128)}, bf16[1,6,2048]{2,1,0:T(8,128)(2,1)S(1)}, bf16[2,133,2048]{2,1,0:T(8,128)(2,1)S(1)}, s32[]{:T(128)}, bf16[8,1]{0,1:T(2,128)(2,1)S(1)...) while((s32[]{:T(128)}, ...), condition=%wide.region_1.2_spmd.clone, body=%wide.region_0.1_spmd.clone.sunk | while | flops 1671319 | bytes 5571106 | solution.py:25
  104.6 12.0 multiply_add_fusion
  119.6 502.0 %while.92 = (s32[]{:T(128)}, f32[320,2048]{1,0:T(8,128)}, bf16[128,2048]{1,0:T(8,128)(2,1)S(1)}, bf16[447,2048]{1,0:T(8,128)(2,1)S(1)}, s32[]{:T(128)}, /*index=5*/s32[]{:T(128)}, s32[]{:T(128)}, s32[]{:T(128)}) while((s32[]{:T(128)}, f32[320,2048]{1,0:T(8,128)}, bf16[128,2048]{1,0:T(8,128)(2,1)S(1)}, ...), condition=%wide.region_3.4_spmd.clone, body=%wide.region_2.3_spmd.clone.sunk | while | flops 2623495 | bytes 6574229 | solution.py:35
  125.8 3.9 select_add_fusion.4
  133.6 3.9 select_add_fusion.4
  141.5 3.9 select_add_fusion.4
  149.4 3.9 select_add_fusion.4
  157.2 3.9 select_add_fusion.4
  165.1 3.9 select_add_fusion.4
  173.0 3.9 select_add_fusion.4
  184.8 3.9 select_add_fusion.4
  192.7 3.9 select_add_fusion.4
  200.5 3.9 select_add_fusion.4
  208.4 3.9 select_add_fusion.4
  622.5 8.4 fusion.35
  631.9 504.0 %while.90 = (s32[]{:T(128)}, f32[128,2048]{1,0:T(8,128)}, bf16[320,2048]{1,0:T(8,128)(2,1)S(1)}, s32[128]{0:T(128)S(1)}, bf16[447,2048]{1,0:T(8,128)(2,1)S(1)}, ...) while((s32[]{:T(128)}, f32[128,2048]{1,0:T(8,128)}, bf16[320,2048]{1,0:T(8,128)(2,1)S(1)}, ...), condition=%wide.region_12.13_spmd, body=%wide.region_10.12_spmd.sunk | while | flops 2619398 | bytes 2646175 | solution.py:59
  1138.3 4.1 pad_maximum_fusion
  1142.4 4.9 reverse.1
  1147.3 21.0 %while.93 = (s32[]{:T(128)}, bf16[127,2048]{1,0:T(8,128)(2,1)S(1)}, s32[]{:T(128)}, bf16[8,1]{0,1:T(2,128)(2,1)S(1)}, bf16[8,127,2048]{2,1,0:T(8,128)(2,1)}, /*index=5*/s32[]{:T(128)}, s32[]{:T(128)}, s32[]{:T(128)}, s32[]{:T(128)}) while((s32[]{:T(128)}, bf16[127,2048]{1,0:T(8,128)(2,1)S(1)}, s32[]{:T(128)}, ...), condition=%wide.region_5.6_spmd.clone, body=%wide.region_4.5_spmd.clone.sunk | while | flops 780424 | bytes 2601399 | solution.py:25
  1171.6 426.0 %while.94 = (s32[]{:T(128)}, f32[320,2048]{1,0:T(8,128)S(1)}, bf16[128,2048]{1,0:T(8,128)(2,1)}, bf16[447,2048]{1,0:T(8,128)(2,1)}, s32[]{:T(128)}, /*index=5*/s32[]{:T(128)}) while((s32[]{:T(128)}, f32[320,2048]{1,0:T(8,128)S(1)}, bf16[128,2048]{1,0:T(8,128)(2,1)}, bf16[447,2048]{1,0:T(8,128)(2,1)}, s32[]{:T(128)}, ...), condition=%wide.region_7.8_spmd.clone, body=%wide.region_6.7_spmd.clone.sunk | while | flops 2623491 | bytes 6574167 | solution.py:46
  1605.1 9.6 fusion.14
  1616.4 12.1 all-gather.3
  1628.6 9.9 while.95
  1638.5 4.7 concatenate.52
  1644.8 30.5 %all-reduce.14.cloned.1.call-done = f32[149,2048]{1,0:T(8,128)} async-done(((f32[149,2048]{1,0:T(8,128)}), f32[149,2048]{1,0:T(8,128)}) %all-reduce.14.cloned.1.call-update) | async-done | bytes 1220624 | tf_op jit(solution)/shard_map/psum | solution.py:208
  1677.6 19.5 %fusion.15 = bf16[3,1,320,2048]{3,2,1,0:T(8,128)(2,1)} fusion(bf16[3,326,2048]{2,1,0:T(8,128)(2,1)} %dynamic_update_slice.14, f32[3,2048]{1,0:T(4,128)S(1)} %get-tuple-element.871, f32[3,2048]{1,0:T(4,128)S(1)} %get-tuple-element.872, f32[3,2048]{1,0:T(4,128)S(1)} %get-tuple-element.873, f32[3,2048]{1,0:T(4,128)S(1)} %get-tuple-element.874, ...), kind=kLoop, calls=%fused_computation.59 | loop fusion | flops 43253760 | bytes 31629632
  1697.1 12.2 psum.15
  (1094 shorter events, 1302.0 us)
Async XLA Ops:
  7.2 70.4 %all-gather.8.cloned.1.call-start = ((), (), s32[]{:S(2)}) async-start(), calls=%async_computation.1 | async-start | bytes 10027008 | tf_op jit(solution)/shard_map/all_gather | solution.py:13
  7.9 2.5 copy-start.12
  10.4 1.9 copy-start.4
  12.5 20.0 %copy-start.5 = (bf16[2,320,2048]{2,1,0:T(8,128)(2,1)}, bf16[2,320,2048]{2,1,0:T(8,128)(2,1)S(1)}, u32[]{:S(2)}) copy-start(bf16[2,320,2048]{2,1,0:T(8,128)(2,1)S(1)} %slice.253) | copy-start | bytes 7864324
  12.5 1.8 copy-start.17
  12.5 22.5 %copy-start.14 = (bf16[3,7,256]{2,1,0:T(8,128)(2,1)S(1)}, bf16[3,7,256]{2,1,0:T(8,128)(2,1)}, u32[]{:S(2)}) copy-start(bf16[3,7,256]{2,1,0:T(8,128)(2,1)} %param.20) | copy-start | bytes 32260
  14.2 42.0 %copy-start.11 = (bf16[128,256]{1,0:T(8,128)(2,1)S(1)}, bf16[128,256]{1,0:T(8,128)(2,1)}, u32[]{:S(2)}) copy-start(bf16[128,256]{1,0:T(8,128)(2,1)} %param.21) | copy-start | bytes 196612
  14.2 1128.1 %all-gather.10.cloned.1.call-start = ((), (), s32[]{:S(2)}) async-start(), calls=%async_computation.2 | async-start | bytes 4718592 | tf_op jit(solution)/shard_map/all_gather | solution.py:13
  103.6 1.0 copy-start.3
  116.7 2.9 copy-start.2
  621.7 0.8 copy-start.10
  631.7 1043.6 %all-reduce.14.cloned.1.call-start = ((), (), s32[]{:S(2)}) async-start(), calls=%async_computation | async-start | bytes 2490368 | tf_op jit(solution)/shard_map/psum | solution.py:208
  1142.4 4.9 copy-start.6
  1142.4 4.9 copy-start.16
  1147.3 24.3 %copy-start.1 = (f32[320,2048]{1,0:T(8,128)S(1)}, f32[320,2048]{1,0:T(8,128)}, u32[]{:S(2)}) copy-start(f32[320,2048]{1,0:T(8,128)} %custom-call.4) | copy-start | bytes 7864324
  1171.6 426.0 %copy-start.13 = (pred[320]{0:T(512)(128)(4,1)S(1)}, pred[320]{0:T(512)(128)(4,1)}, u32[]{:S(2)}) copy-start(pred[320]{0:T(512)(128)(4,1)} %copy-done.12) | copy-start | bytes 964
  1597.6 3.9 copy-start.8
  1597.6 6.1 copy-start.7
  1601.4 3.6 copy-start
  1605.1 10.1 copy-start.9
  1614.7 1.7 slice-start
  1614.8 13.8 copy-start.15
Sparse Core Ops, SparseCore 0:
  14.4 63.1 all-gather.7
  631.8 36.7 all-gather.9
  1616.5 58.7 all-reduce.13
where the time goes:
time: 1750 us; the launch traced here: 1720 us
  other arithmetic  1090 us (62%)
  local copies, waits for them, and re-layouts  316 us (18%)
  loops' own time  185 us (11%)
  blocking collectives  74.1 us (4%)
  waiting for transfers between devices  35.5 us (2%)
    add x128, other arithmetic, causal_add_tap(): total + filt[tap_index].astype(jnp.float32)[None, :] * piece.astype(jnp.f...  499 us
    add x128, other arithmetic, anticausal_add_tap(): total + filt[tap_index].astype(jnp.float32)[None, :] * piece.astype(jnp.f...  325 us
    dynamic_update_slice x128, local copies, waits for them, and re-layouts, tap_products(): return lax.map(one_tap, jnp.arange(taps, dtype=jnp.int32))  192 us
    another operation x1, loops' own time, tap_products(): return lax.map(one_tap, jnp.arange(taps, dtype=jnp.int32))  168 us
    mul x128, other arithmetic, anticausal_add_tap(): filt[tap_index].astype(jnp.float32)[None, :] * piece.astype(jnp.float32)  98.6 us
    dynamic_slice x128, local copies, waits for them, and re-layouts, tap_products(): return lax.map(one_tap, jnp.arange(taps, dtype=jnp.int32))  74.5 us
    reduce_sum x128, other arithmetic, one_tap(): jnp.sum(grad_rows.astype(jnp.float32) * piece.astype(jnp.float32), axis=0)  69.5 us
  transfers between devices with their start and end apart: 3, of which 2 were waited for; matrix products, arithmetic and copies ran while one was open for 21% of the time, Pallas kernels for 0%

commit v1 on v0

v1 whole, which is shorter than its diff:
```python
import functools

import jax
import jax.numpy as jnp
import numpy as np
from jax import lax
from jax.experimental import pallas as pl
from jax.experimental.pallas import tpu as pltpu
from jax.sharding import PartitionSpec as P

CH = 8192
LTAP = 128
STAP = 7
MEAN_COUNT = 256
REACH = LTAP - 1 + STAP - 1
N = 480
HALF = N // 2
LEAD = 136
TRAIL = 464
SHORT = 336
ZLEAD = 128
GROWS = 152
F32 = jnp.float32
BF16 = jnp.bfloat16


def ceil16(rows):
    return -(-rows // 16) * 16


def halo_plan(devices, cap):
    slack = devices * cap - devices * MEAN_COUNT
    plan = []
    for distance in range(1, devices):
        nearer = max(distance - 1, (distance - 1) * cap - slack)
        if nearer >= REACH:
            break
        big = ceil16(REACH - nearer)
        small = 16 if nearer < STAP - 1 else 0
        plan.append((big, small))
    return plan


def split(matrix):
    high = matrix.astype(BF16)
    low = (matrix - high.astype(np.float64)).astype(BF16)
    return high, low


def transforms():
    freq = (2.0 * np.pi / N) * (np.arange(HALF) + 0.5)[:, None]

    def forward(first, rows):
        angle = freq * (first + np.arange(rows))[None, :]
        return np.concatenate([np.cos(angle), -np.sin(angle)], axis=0)

    back = forward(0, SHORT).T * (2.0 / N)
    return split(forward(-ZLEAD, TRAIL)) + split(forward(0, TRAIL)) + split(back)


def dot(a, b):
    return jnp.dot(a, b, preferred_element_type=F32)


def chunks(rows, size=32):
    return [(start, min(size, rows - start)) for start in range(0, rows, size)]


def block_kernel(plan, cap, info, *refs):
    tails = refs[: len(plan)]
    heads = refs[len(plan) : 2 * len(plan)]
    refs = refs[2 * len(plan) :]
    (streams, dy_in, filt, fz_hi, fz_lo, fd_hi, fd_lo, g_hi, g_lo) = refs[:9]
    grads_out, sums_out = refs[9:11]
    refs = refs[11:]
    (kw, vw, qw, dyw, ks, vs, zs, dyl, dyl_own, zh, hh, dh, dho, p_hi, p_lo, yz, dm) = refs[:17]
    before = refs[17 : 17 + len(plan)]
    after = refs[17 + len(plan) : 17 + 2 * len(plan)]
    before_q = refs[17 + 2 * len(plan)]
    cols = streams.shape[-1]
    count = info[0]
    remaining = info[1]

    @pl.when(pl.program_id(0) == 0)
    def _():
        for at, (big, small) in enumerate(plan):
            base, live = info[2 + 4 * at], info[3 + 4 * at]
            col = lax.broadcasted_iota(jnp.int32, (LEAD, big), 1)
            row = lax.broadcasted_iota(jnp.int32, (LEAD, big), 0)
            hit = (row - LEAD == col - big - base) & (big - col <= live)
            before[at][...] = jnp.where(hit, 1.0, 0.0).astype(BF16)
            if small:
                col = lax.broadcasted_iota(jnp.int32, (16, 16), 1)
                row = lax.broadcasted_iota(jnp.int32, (16, 16), 0)
                hit = (row == col - base) & (16 - col <= live)
                before_q[at] = jnp.where(hit, 1.0, 0.0).astype(BF16)
            base, live = info[4 + 4 * at], info[5 + 4 * at]
            col = lax.broadcasted_iota(jnp.int32, (TRAIL, big), 1)
            row = lax.broadcasted_iota(jnp.int32, (TRAIL, big), 0)
            hit = (row == col + base) & (col < live)
            after[at][...] = jnp.where(hit, 1.0, 0.0).astype(BF16)

    with jax.named_scope("windows"):
        for which, window in ((0, kw), (1, vw)):
            lead = None
            trail = None
            for at, (big, small) in enumerate(plan):
                part = dot(before[at][...], tails[at][which * big : (which + 1) * big, :])
                lead = part if lead is None else lead + part
                if small:
                    first = 2 * big + which * 16
                    part = dot(after[at][:SHORT, :16], heads[at][first : first + 16, :])
                    trail = part if trail is None else trail + part
            window[:LEAD, :] = lead
            window[LEAD:, :] = trail
            for start, size in chunks(cap):
                row = lax.broadcasted_iota(jnp.int32, (size, 1), 0) + start
                own = streams[1 + which, 0, start : start + size, :].astype(F32)
                window[LEAD + start : LEAD + start + size, :] += jnp.where(row < count, own, 0.0)
        lead = None
        for at, (big, small) in enumerate(plan):
            if small:
                part = dot(before_q[at], tails[at][2 * big : 2 * big + 16, :])
                lead = part if lead is None else lead + part
        qw[:8, :] = lead[8:]
        for which, window, first in ((0, qw, 8), (1, dyw, 0)):
            trail = None
            for at, (big, small) in enumerate(plan):
                part = dot(after[at][...], heads[at][which * big : (which + 1) * big, :])
                trail = part if trail is None else trail + part
            window[first:, :] = trail
            for start, size in chunks(cap):
                row = lax.broadcasted_iota(jnp.int32, (size, 1), 0) + start
                source = streams[0, 0, start : start + size, :] if which == 0 else dy_in[0, start : start + size, :]
                window[first + start : first + start + size, :] += jnp.where(
                    row < count, source.astype(F32), 0.0
                )

    taps = filt[LTAP : LTAP + 32, :].astype(F32)

    def tap(stream, index):
        at = stream * STAP + index
        return taps[at : at + 1, :]

    def causal(window, stream, start, size):
        rows = window[start : start + size + 8, :]
        total = tap(stream, 0) * rows[8:, :]
        for index in range(1, STAP):
            total = total + tap(stream, index) * rows[8 - index : 8 - index + size, :]
        return total

    with jax.named_scope("short_forward"):
        for start, size in chunks(TRAIL):
            span = slice(start, start + size)
            keys = causal(kw, 1, start, size)
            values = causal(vw, 2, start, size)
            ks[span, :] = keys
            vs[span, :] = values
            zs[span, :] = (keys * values).astype(BF16)
        for start, size in chunks(TRAIL):
            span = slice(start, start + size)
            grad = (dyw[span, :] * causal(qw, 0, start, size)).astype(BF16)
            dyl[span, :] = grad
            if start < cap:
                row = lax.broadcasted_iota(jnp.int32, (size, 1), 0) + start
                dyl_own[span, :] = jnp.where(row < count, grad.astype(F32), 0.0).astype(BF16)

    with jax.named_scope("transforms"):
        long = filt[:LTAP, :]
        zh[...] = dot(fz_hi[...], zs[...]) + dot(fz_lo[...], zs[...])
        hh[...] = dot(fd_hi[:, :LTAP], long) + dot(fd_lo[:, :LTAP], long)
        dh[...] = dot(fd_hi[...], dyl[...]) + dot(fd_lo[...], dyl[...])
        dho[...] = dot(fd_hi[:, :cap], dyl_own[...]) + dot(fd_lo[:, :cap], dyl_own[...])

    def product(a, b, conjugate):
        for start, size in chunks(HALF, 16):
            real, imag = slice(start, start + size), slice(HALF + start, HALF + start + size)
            ar, ai, br, bi = a[real, :], a[imag, :], b[real, :], b[imag, :]
            if conjugate:
                cr, ci = ar * br + ai * bi, ai * br - ar * bi
            else:
                cr, ci = ar * br - ai * bi, ai * br + ar * bi
            for span, part in ((real, cr), (imag, ci)):
                high = part.astype(BF16)
                p_hi[span, :] = high
                p_lo[span, :] = (part - high.astype(F32)).astype(BF16)

    def inverse(rows):
        return (
            dot(g_hi[:rows, :], p_hi[...])
            + dot(g_lo[:rows, :], p_hi[...])
            + dot(g_hi[:rows, :], p_lo[...])
        )

    with jax.named_scope("long_filter_grad"):
        product(dho, zh, True)
        sums_out[:LTAP, :] = inverse(LTAP)

    with jax.named_scope("long_forward"):
        product(zh, hh, False)
        yz[...] = inverse(SHORT)
        for start, size in chunks(SHORT):
            span = slice(start, start + size)
            dm[0, span, :] = (dyw[span, :] * yz[span, :]).astype(BF16).astype(F32)

    with jax.named_scope("long_backward"):
        product(dh, hh, True)
        yz[...] = inverse(SHORT)
        for start, size in chunks(SHORT):
            span = slice(start, start + size)
            own = slice(ZLEAD + start, ZLEAD + start + size)
            row = lax.broadcasted_iota(jnp.int32, (size, 1), 0) + start
            grad = jnp.where(row < remaining, yz[span, :], 0.0)
            dm[1, span, :] = (grad * vs[own, :]).astype(BF16).astype(F32)
            dm[2, span, :] = (grad * ks[own, :]).astype(BF16).astype(F32)

    with jax.named_scope("short_backward"):
        for stream, window, lead in ((0, qw, 8), (1, kw, LEAD), (2, vw, LEAD)):
            partial = [jnp.zeros((8, cols), F32) for _ in range(STAP)]
            for start, size in chunks(cap):
                row = lax.broadcasted_iota(jnp.int32, (size, 1), 0) + start
                rows = dm[stream, start : start + size + 8, :]
                total = tap(stream, 0) * rows[:size, :]
                for index in range(1, STAP):
                    total = total + tap(stream, index) * rows[index : index + size, :]
                grads_out[stream, 0, start : start + size, :] = jnp.where(
                    row < count, total, 0.0
                ).astype(BF16)
                mine = jnp.where(row < count, rows[:size, :], 0.0)
                source = window[lead + start - 8 : lead + start + size, :]
                for index in range(STAP):
                    terms = mine * source[8 - index : 8 - index + size, :]
                    for at in range(0, size, 8):
                        partial[index] = partial[index] + terms[at : at + 8, :]
            for index in range(STAP):
                at = LTAP + stream * STAP + index
                sums_out[at : at + 1, :] = jnp.sum(partial[index], axis=0, keepdims=True)
        used = LTAP + 3 * STAP
        sums_out[used:, :] = jnp.zeros((GROWS - used, cols), F32)


def run_blocks(plan, info, tails, heads, streams, cotangent, filters, width=256):
    cap, channels = streams.shape[2:]
    width = min(width, channels)
    matrices = transforms()

    def by_block(rows):
        return pl.BlockSpec((rows, width), lambda step: (0, step))

    whole = [pl.BlockSpec(matrix.shape, lambda step: (0, 0)) for matrix in matrices]
    f32_rows = [
        LEAD + SHORT, LEAD + SHORT, 8 + TRAIL, TRAIL, TRAIL, TRAIL,
    ]
    scratch = [pltpu.VMEM((rows, width), F32) for rows in f32_rows]
    scratch += [pltpu.VMEM((rows, width), BF16) for rows in (TRAIL, TRAIL, cap)]
    scratch += [pltpu.VMEM((N, width), F32) for _ in range(4)]
    scratch += [pltpu.VMEM((N, width), BF16) for _ in range(2)]
    scratch += [pltpu.VMEM((SHORT, width), F32), pltpu.VMEM((3, SHORT, width), F32)]
    scratch += [pltpu.VMEM((LEAD, big), BF16) for big, _ in plan]
    scratch += [pltpu.VMEM((TRAIL, big), BF16) for big, _ in plan]
    scratch += [pltpu.VMEM((len(plan), 16, 16), BF16)]
    return pl.pallas_call(
        functools.partial(block_kernel, plan, cap),
        grid=(channels // width,),
        in_specs=[pl.BlockSpec(memory_space=pltpu.SMEM)]
        + [by_block(part.shape[0]) for part in tails + heads]
        + [
            pl.BlockSpec((3, 1, cap, width), lambda step: (0, 0, 0, step)),
            pl.BlockSpec((1, cap, width), lambda step: (0, 0, step)),
            by_block(filters.shape[0]),
        ]
        + whole,
        out_specs=[
            pl.BlockSpec((3, 1, cap, width), lambda step: (0, 0, 0, step)),
            by_block(GROWS),
        ],
        out_shape=[
            jax.ShapeDtypeStruct(streams.shape, BF16),
            jax.ShapeDtypeStruct((GROWS, channels), F32),
        ],
        scratch_shapes=scratch,
        compiler_params=pltpu.CompilerParams(vmem_limit_bytes=48 * 1024 * 1024),
        name="hyena_blocks",
    )(info, *tails, *heads, streams, cotangent, filters, *[jnp.asarray(m) for m in matrices])


def last_rows(block, live_count, length):
    zero_rows = jnp.zeros(block.shape[:-2] + (length, block.shape[-1]), block.dtype)
    padded = jnp.concatenate([zero_rows, block], axis=-2)
    return lax.dynamic_slice_in_dim(padded, live_count, length, axis=block.ndim - 2)


def halo_info(counts, me, plan):
    devices = counts.shape[0]
    ids = jnp.arange(devices, dtype=jnp.int32)

    def total(first, end):
        return jnp.sum(jnp.where((ids >= first) & (ids < end), counts, 0))

    numbers = [total(me, me + 1), total(me, devices)]
    for distance in range(1, len(plan) + 1):
        numbers += [
            total(me - distance + 1, me),
            total(me - distance, me - distance + 1),
            total(me, me + distance),
            total(me + distance, me + distance + 1),
        ]
    return jnp.stack(numbers).astype(jnp.int32)


def local(streams, cotangent, counts, short_filters, long_filter):
    devices = lax.axis_size("ctx")
    me = lax.axis_index("ctx")
    live_count = counts[0, 0]
    cap = streams.shape[2]
    share = long_filter.shape[1]
    plan = halo_plan(devices, cap)
    q0, k0, v0 = streams[0, 0], streams[1, 0], streams[2, 0]
    dy = cotangent[0]
    digits = jnp.stack([live_count // 16, live_count % 16]).astype(BF16)
    packed = jnp.concatenate(
        [
            long_filter,
            short_filters.reshape(3 * STAP, share),
            jnp.broadcast_to(digits[:, None], (2, share)),
            jnp.zeros((160 - LTAP - 3 * STAP - 2, share), BF16),
        ],
        axis=0,
    )
    filters = lax.all_gather(packed, "ctx", axis=1, tiled=True)
    digits = filters[LTAP + 3 * STAP : LTAP + 3 * STAP + 2, ::share].astype(jnp.int32)
    info = halo_info(digits[0] * 16 + digits[1], me, plan)
    widest = plan[0][0]
    tail = last_rows(streams[:, 0], live_count, widest)
    tails, heads = [], []
    for at, (big, small) in enumerate(plan):
        distance = at + 1
        later = [(j, j + distance) for j in range(devices - distance)]
        earlier = [(j + distance, j) for j in range(devices - distance)]
        last = [tail[1, widest - big :], tail[2, widest - big :]]
        first = [q0[:big], dy[:big]]
        if small:
            last.append(tail[0, widest - small :])
            first += [k0[:small], v0[:small]]
        tails.append(lax.ppermute(jnp.concatenate(last, axis=0), "ctx", later))
        heads.append(lax.ppermute(jnp.concatenate(first, axis=0), "ctx", earlier))
    stream_grads, sums = run_blocks(plan, info, tails, heads, streams, cotangent, filters)
    own = lax.psum_scatter(sums, "ctx", scatter_dimension=1, tiled=True)
    squares = lax.psum(jnp.sum(own * own), ("dp", "ctx"))
    rms = jnp.sqrt(squares / float((LTAP + 3 * STAP) * CH) + 1e-06)
    normed = own / rms
    long_grad = normed[:LTAP]
    short_grad = normed[LTAP : LTAP + 3 * STAP].reshape(3, STAP, share)
    return (stream_grads, long_grad, short_grad)


def solution(mesh):
    return jax.shard_map(
        local,
        mesh=mesh,
        in_specs=(
            P(None, None, "ctx", "dp"),
            P(None, "ctx", "dp"),
            P(None, "ctx"),
            P(None, None, ("dp", "ctx")),
            P(None, ("dp", "ctx")),
        ),
        out_specs=(
            P(None, None, "ctx", "dp"),
            P(None, ("dp", "ctx")),
            P(None, None, ("dp", "ctx")),
        ),
        check_vma=False,
    )
```

time: 1750 us -> 263 us (0.15); the launches traced: 1720 us -> 263 us
  other arithmetic: 1090 us -> 6.6 us
  local copies, waits for them, and re-layouts: 316 us -> 18 us
  loops' own time: 185 us -> 0 us
  Pallas kernels: 0 us -> 44.9 us
  blocking collectives: 74.1 us -> 108 us
    add x257 -> x0, other arithmetic: 836 us -> none  [the longest x128 499 us: causal_add_tap(): total + filt[tap_index].astype(jnp.float32)[None, :] * piece.astype(jnp.f...]
    dynamic_update_slice x130 -> x0, local copies, waits for them, and re-layouts: 197 us -> none  [the longest x128 192 us: tap_products(): return lax.map(one_tap, jnp.arange(taps, dtype=jnp.int32))]
    another operation x6 -> x0, loops' own time: 185 us -> none  [the longest x1 168 us: tap_products(): return lax.map(one_tap, jnp.arange(taps, dtype=jnp.int32))]
    mul x259 -> x0, other arithmetic: 101 us -> none  [the longest x128 98.6 us: anticausal_add_tap(): filt[tap_index].astype(jnp.float32)[None, :] * piece.astype(jnp.float32)]
    dynamic_slice x151 -> x0, local copies, waits for them, and re-layouts: 89.2 us -> none  [the longest x128 74.5 us: tap_products(): return lax.map(one_tap, jnp.arange(taps, dtype=jnp.int32))]
    reduce_sum x130 -> x2, other arithmetic: 81.3 us -> 2.46 us  [the longest x1 1.56 us: local(): squares = lax.psum(jnp.sum(own * own), ('dp', 'ctx'))]
    pallas_call x0 -> x1, Pallas kernels: none -> 44.9 us  [run_blocks(): pl.pallas_call(functools.partial(block_kernel, plan, cap), grid=(channels...]
    reduce_scatter x0 -> x1, waiting for transfers between devices: none -> 36.7 us  [local(): own = lax.psum_scatter(sums, 'ctx', scatter_dimension=1, tiled=True)]
  transfers between devices with their start and end apart: 3 -> 7, of which waited for: 2 -> 2; matrix products, arithmetic and copies ran while one was open for 21% -> 5% of each run, Pallas kernels for 0% -> 0%
where the time goes in v1:
time: 263 us
  blocking collectives  108 us (41%)
  waiting for transfers between devices  52.4 us (20%)
  Pallas kernels  44.9 us (17%)
  local copies, waits for them, and re-layouts  18 us (7%)
  starting transfers between devices  16.8 us (6%)
  between operations  15.7 us (6%)
  other arithmetic  6.6 us (3%)
    all_gather x1, blocking collectives, local(): filters = lax.all_gather(packed, 'ctx', axis=1, tiled=True)  68.8 us
    pallas_call x1, Pallas kernels, run_blocks(): pl.pallas_call(functools.partial(block_kernel, plan, cap), grid=(channels...  44.9 us
    psum x1, blocking collectives, local(): squares = lax.psum(jnp.sum(own * own), ('dp', 'ctx'))  39.5 us
    reduce_scatter x1, waiting for transfers between devices, local(): own = lax.psum_scatter(sums, 'ctx', scatter_dimension=1, tiled=True)  36.7 us
    ppermute x3, waiting for transfers between devices, local(): tails.append(lax.ppermute(jnp.concatenate(last, axis=0), 'ctx', later))  15.7 us
    ppermute x3, starting transfers between devices, local(): tails.append(lax.ppermute(jnp.concatenate(last, axis=0), 'ctx', later))  12.9 us
    another operation x1, local copies, waits for them, and re-layouts, halo_info(): return jnp.stack(numbers).astype(jnp.int32)  8.83 us
  transfers between devices with their start and end apart: 7, of which 2 were waited for; matrix products, arithmetic and copies ran while one was open for 5% of the time, Pallas kernels for 0%

profile of v1, /device:TPU:0, one launch (start us, length us, event | category | flops | bytes accessed | tf_op | source)
XLA Modules:
  0.0 262.6 jit_solution(10727688047600789059)
XLA Ops:
  7.9 1.8 fusion
  9.7 0.6 copy-done.6
  10.4 0.1 fusion.4
  10.4 1.2 pad_maximum_fusion.1
  11.6 5.9 %collective-permute-start.1 = (bf16[304,2048]{1,0:T(8,128)(2,1)}, bf16[304,2048]{1,0:T(8,128)(2,1)}, u32[]{:S(2)}, u32[]{:S(2)}) collective-permute-start(bf16[304,2048]{1,0:T(8,128)(2,1)} %pad_maximum_fusion.1), channel_id=1, source_target_pairs={{0,2},{1,3},{2,4},{3,5},{4,6},{5,7},{8,10},{9,11},{10,12},{11,13},... | collective-permute-start | bytes 3735560 | tf_op jit(solution)/shard_map/ppermute | solution.py:345
  17.5 1.5 collective-permute-start
  19.2 1.2 slice_bitcast_fusion
  20.4 1.1 pad_maximum_fusion
  21.6 1.3 collective-permute-start.4
  22.9 1.3 collective-permute-start.3
  24.2 5.4 %collective-permute-start.2 = (bf16[32,2048]{1,0:T(8,128)(2,1)S(1)}, bf16[32,2048]{1,0:T(8,128)(2,1)S(1)}, u32[]{:S(2)}, u32[]{:S(2)}) collective-permute-start(bf16[32,2048]{1,0:T(8,128)(2,1)S(1)} %pad_maximum_fusion.2), channel_id=1, source_target_pairs={{0,3},{1,4},{2,5},{3,6},{4,7},{8,11},{9,12},{10,13},{11,14},{12,15... | collective-permute-start | bytes 393224 | tf_op jit(solution)/shard_map/ppermute | solution.py:345
  29.7 0.1 pad.15.clone
  29.8 0.1 pad_maximum_fusion.4
  29.9 0.8 slice_bitcast_fusion.2
  30.7 0.7 pad_maximum_fusion.3
  31.4 0.1 maximum_maximum_fusion
  31.5 15.7 %collective-permute-done.2.refs_2_ = bf16[32,2048]{1,0:T(8,128)(2,1)S(1)} collective-permute-done((bf16[32,2048]{1,0:T(8,128)(2,1)S(1)}, bf16[32,2048]{1,0:T(8,128)(2,1)S(1)}, u32[]{:S(2)}, u32[]{:S(2)}) %collective-permute-start.2) | collective-permute-done | bytes 131104 | tf_op jit(solution)/shard_map/ppermute | solution.py:345
  47.2 1.3 collective-permute-start.5
  48.5 68.8 %all_gather.3.refs_8_ = bf16[160,2048]{1,0:T(8,128)(2,1)S(1)} all-gather(bf16[160,256]{1,0:T(8,128)(2,1)S(1)} %maximum_maximum_fusion), channel_id=1, replica_groups=mesh['dp'=4,'ctx'=8] {'ctx'}, dimensions={1}, use_global_device_ids=true | all-gather | bytes 737280 | tf_op jit(solution)/shard_map/all_gather | solution.py:330
  117.3 0.1 slice.80
  117.4 0.9 fusion.6
  118.3 8.8 %stack.65.info = s32[14]{0:T(128)S(1)} concatenate(s32[1]{0:T(128)} %bitcast.4, s32[1]{0:T(128)} %bitcast.5, s32[1]{0:T(128)} %bitcast.6, s32[1]{0:T(128)} %bitcast.7, s32[1]{0:T(128)} %bitcast.4, s32[1]{0:T(128)} %bitcast.8, s32[1]{0:T(128)} %bitcast.7, s32[1]{0:T(128)} %bitcast.9, s32[1]{0:T(128)} %bitcast.10, s32[1]{0:T(128)} %bitcast.11, s32[1]{0:T(128)} %bitcast.12, ...), dimensions={0} | concatenate | bytes 112 | tf_op jit(solution)/shard_map/stack | solution.py:308
  127.3 1.0 copy-done.3
  128.3 1.0 copy-done.4
  129.3 1.0 copy-done.5
  130.2 44.9 %hyena_blocks.1 = (bf16[3,1,320,2048]{3,2,1,0:T(8,128)(2,1)}, f32[152,2048]{1,0:T(8,128)}) custom-call(s32[14]{0:T(128)S(1)} %stack.65.info, bf16[304,2048]{1,0:T(8,128)(2,1)S(1)} %collective-permute-done.refs_0_, bf16[304,2048]{1,0:T(8,128)(2,1)} %collective-permute-done.1.refs_1_, bf16[32,2048]{1,0:T(8,128)(2,1)S(1)} %collective-permute-done.2.refs_2_, ...), custom_call_target="tpu_custom_call" | custom-call | tf_op jit(solution)/shard_map/hyena_blocks/pallas_call | solution.py:262
  175.1 36.7 %reduce-scatter.2.cloned.1.call-done = f32[152,256]{1,0:T(8,128)} async-done(((f32[152,2048]{1,0:T(8,128)}), f32[152,256]{1,0:T(8,128)}) %reduce-scatter.2.cloned.1.call-update) | async-done | bytes 155664 | tf_op jit(solution)/shard_map/reduce_scatter | solution.py:348
  211.8 1.6 multiply_reduce_fusion
  213.4 39.5 %psum.7 = f32[]{:T(128)} all-reduce(f32[]{:T(128)} %multiply_reduce_fusion), channel_id=1, replica_groups=mesh['dp'=4,'ctx'=8] {'dp','ctx'}, use_global_device_ids=true, to_apply=%region_14.15 | all-reduce | flops 1 | bytes 8 | tf_op jit(solution)/shard_map/psum | solution.py:349
  253.6 0.9 broadcast_divide_fusion
  254.5 0.7 slice.102
  255.2 0.6 reshape.41
  (28 shorter events, 0.2 us)
Async XLA Ops:
  7.2 204.6 %reduce-scatter.2.cloned.1.call-start = ((), (), s32[]{:S(2)}) async-start(), calls=%async_computation.1 | async-start | bytes 1400832 | tf_op jit(solution)/shard_map/reduce_scatter | solution.py:348
  7.9 2.5 copy-start.6
  11.6 115.5 %collective-permute-start.1 = (bf16[304,2048]{1,0:T(8,128)(2,1)}, bf16[304,2048]{1,0:T(8,128)(2,1)}, u32[]{:S(2)}, u32[]{:S(2)}) collective-permute-start(bf16[304,2048]{1,0:T(8,128)(2,1)} %pad_maximum_fusion.1), channel_id=1, source_target_pairs={{0,2},{1,3},{2,4},{3,5},{4,6},{5,7},{8,10},{9,11},{10,12},{11,13},... | collective-permute-start | bytes 3735560 | tf_op jit(solution)/shard_map/ppermute | solution.py:345
  17.5 109.7 %collective-permute-start = (bf16[304,2048]{1,0:T(8,128)(2,1)}, bf16[304,2048]{1,0:T(8,128)(2,1)S(1)}, u32[]{:S(2)}, u32[]{:S(2)}) collective-permute-start(bf16[304,2048]{1,0:T(8,128)(2,1)} %pad_maximum_fusion.1), channel_id=1, source_target_pairs={{0,1},{1,2},{2,3},{3,4},{4,5},{5,6},{6,7},{8,9},{9,10},{10,11},{11... | collective-permute-start | bytes 3735560 | tf_op jit(solution)/shard_map/ppermute | solution.py:345
  19.1 10.6 %copy-start.8 = (bf16[3,7,256]{2,1,0:T(8,128)(2,1)S(1)}, bf16[3,7,256]{2,1,0:T(8,128)(2,1)}, u32[]{:S(2)}) copy-start(bf16[3,7,256]{2,1,0:T(8,128)(2,1)} %param.14) | copy-start | bytes 32260
  19.2 12.2 %copy-start.7 = (bf16[128,256]{1,0:T(8,128)(2,1)S(1)}, bf16[128,256]{1,0:T(8,128)(2,1)}, u32[]{:S(2)}) copy-start(bf16[128,256]{1,0:T(8,128)(2,1)} %param.15) | copy-start | bytes 196612
  19.2 108.0 %copy-start = (bf16[480,464]{1,0:T(8,128)(2,1)S(1)}, bf16[480,464]{1,0:T(8,128)(2,1)}, u32[]{:S(2)}) copy-start(bf16[480,464]{1,0:T(8,128)(2,1)} %constant.77.clone.refs_12_) | copy-start | bytes 1336324
  19.2 108.0 %copy-start.1 = (bf16[480,464]{1,0:T(8,128)(2,1)S(1)}, bf16[480,464]{1,0:T(8,128)(2,1)}, u32[]{:S(2)}) copy-start(bf16[480,464]{1,0:T(8,128)(2,1)} %constant.76.clone.refs_11_) | copy-start | bytes 1336324
  19.2 108.0 %copy-start.2 = (bf16[480,464]{1,0:T(8,128)(2,1)S(1)}, bf16[480,464]{1,0:T(8,128)(2,1)}, u32[]{:S(2)}) copy-start(bf16[480,464]{1,0:T(8,128)(2,1)} %constant.75.clone.refs_10_) | copy-start | bytes 1336324
  21.6 105.6 %collective-permute-start.4 = (bf16[320,2048]{1,0:T(8,128)(2,1)}, bf16[320,2048]{1,0:T(8,128)(2,1)}, u32[]{:S(2)}, u32[]{:S(2)}) collective-permute-start(bf16[320,2048]{1,0:T(8,128)(2,1)} %pad_maximum_fusion), channel_id=1, source_target_pairs={{2,0},{3,1},{4,2},{5,3},{6,4},{7,5},{10,8},{11,9},{12,10},{13,11},... | collective-permute-start | bytes 3932168 | tf_op jit(solution)/shard_map/ppermute | solution.py:346
  22.9 104.3 %collective-permute-start.3 = (bf16[320,2048]{1,0:T(8,128)(2,1)}, bf16[320,2048]{1,0:T(8,128)(2,1)}, u32[]{:S(2)}, u32[]{:S(2)}) collective-permute-start(bf16[320,2048]{1,0:T(8,128)(2,1)} %pad_maximum_fusion), channel_id=1, source_target_pairs={{1,0},{2,1},{3,2},{4,3},{5,4},{6,5},{7,6},{9,8},{10,9},{11,10},{12... | collective-permute-start | bytes 3932168 | tf_op jit(solution)/shard_map/ppermute | solution.py:346
  24.2 23.1 %collective-permute-start.2 = (bf16[32,2048]{1,0:T(8,128)(2,1)S(1)}, bf16[32,2048]{1,0:T(8,128)(2,1)S(1)}, u32[]{:S(2)}, u32[]{:S(2)}) collective-permute-start(bf16[32,2048]{1,0:T(8,128)(2,1)S(1)} %pad_maximum_fusion.2), channel_id=1, source_target_pairs={{0,3},{1,4},{2,5},{3,6},{4,7},{8,11},{9,12},{10,13},{11,14},{12,15... | collective-permute-start | bytes 393224 | tf_op jit(solution)/shard_map/ppermute | solution.py:345
  47.2 79.9 %collective-permute-start.5 = (bf16[32,2048]{1,0:T(8,128)(2,1)}, bf16[32,2048]{1,0:T(8,128)(2,1)}, u32[]{:S(2)}, u32[]{:S(2)}) collective-permute-start(bf16[32,2048]{1,0:T(8,128)(2,1)} %pad_maximum_fusion.3), channel_id=1, source_target_pairs={{3,0},{4,1},{5,2},{6,3},{7,4},{11,8},{12,9},{13,10},{14,11},{15,12... | collective-permute-start | bytes 393224 | tf_op jit(solution)/shard_map/ppermute | solution.py:346
  127.2 1.0 copy-start.3
  128.3 1.0 copy-start.4
  129.3 1.0 copy-start.5
Sparse Core Ops, SparseCore 0:
  175.2 36.5 reduce-scatter.1

commit v2 on v1

--- a/solution.py
+++ b/solution.py
@@ -19,7 +19,7 @@
 TRAIL = 464
 SHORT = 336
 ZLEAD = 128
-GROWS = 152
+GROWS = 160
 F32 = jnp.float32
 BF16 = jnp.bfloat16
 
@@ -284,39 +284,264 @@
     )(info, *tails, *heads, streams, cotangent, filters, *[jnp.asarray(m) for m in matrices])
 
 
-def last_rows(block, live_count, length):
-    zero_rows = jnp.zeros(block.shape[:-2] + (length, block.shape[-1]), block.dtype)
-    padded = jnp.concatenate([zero_rows, block], axis=-2)
-    return lax.dynamic_slice_in_dim(padded, live_count, length, axis=block.ndim - 2)
+def axis_copy(source, target, send_sem, recv_sem, axis, device):
+    return pltpu.make_async_remote_copy(
+        src_ref=source,
+        dst_ref=target,
+        send_sem=send_sem,
+        recv_sem=recv_sem,
+        device_id={axis: device},
+        device_id_type=pl.DeviceIdType.MESH,
+    )
+
+
+def greet(axes):
+    barrier = pltpu.get_barrier_semaphore()
+    total = 0
+    for axis in axes:
+        size = lax.axis_size(axis)
+        me = lax.axis_index(axis)
+        for offset in range(1, size):
+            pl.semaphore_signal(
+                barrier,
+                inc=1,
+                device_id={axis: lax.rem(me + offset, size)},
+                device_id_type=pl.DeviceIdType.MESH,
+            )
+        total += size - 1
+    pl.semaphore_wait(barrier, total)
+
+
+def exchange_kernel(plan, devices, count, kept, streams, cotangent, packed, *refs):
+    tails = refs[: len(plan)]
+    heads = refs[len(plan) : 2 * len(plan)]
+    filters, last, zeros, send, recv, filter_send, filter_recv, own_sem, zero_sem = refs[2 * len(plan) :]
+    me = lax.axis_index("ctx")
+    cap, channels = kept.shape[2:]
+    share = packed.shape[1]
+    widest = plan[0][0]
+    gather = filters.shape[1] > share
+    mine = filters.at[:, pl.ds(pl.multiple_of(me * share, share), share)] if gather else filters
+    own = pltpu.make_async_copy(packed, mine, own_sem)
+    own.start()
+    zeros[...] = jnp.zeros_like(zeros)
+
+    head_copies, tail_copies, blanks = [], [], []
+    slot = 0
+    for at, (big, small) in enumerate(plan):
+        distance = at + 1
+        after = jnp.minimum(me + distance, devices - 1)
+        before = jnp.maximum(me - distance, 0)
+        pieces = [
+            (streams.at[0, 0, pl.ds(0, big), :], 0, big),
+            (cotangent.at[0, pl.ds(0, big), :], big, big),
+        ]
+        if small:
+            pieces += [
+                (streams.at[1, 0, pl.ds(0, small), :], 2 * big, small),
+                (streams.at[2, 0, pl.ds(0, small), :], 2 * big + small, small),
+            ]
+        for source, first, rows in pieces:
+            target = heads[at].at[pl.ds(first, rows), :]
+            copy = axis_copy(source, target, send.at[slot], recv.at[slot], "ctx", before)
+            head_copies.append((distance, copy))
+            slot += 1
+        if big == widest and small:
+            pieces = [(last, 0, 2 * widest + small)]
+        else:
+            pieces = [
+                (last.at[pl.ds(widest - big, big), :], 0, big),
+                (last.at[pl.ds(2 * widest - big, big), :], big, big),
+            ]
+            if small:
+                pieces.append((last.at[pl.ds(2 * widest, small), :], 2 * big, small))
+        for source, first, rows in pieces:
+            target = tails[at].at[pl.ds(first, rows), :]
+            copy = axis_copy(source, target, send.at[slot], recv.at[slot], "ctx", after)
+            tail_copies.append((distance, copy))
+            slot += 1
+        rows = tails[at].shape[0]
+        blank = pltpu.make_async_copy(zeros.at[pl.ds(0, rows), :], tails[at], zero_sem.at[2 * at])
+        blanks.append((me < distance, blank))
+        rows = heads[at].shape[0]
+        blank = pltpu.make_async_copy(zeros.at[pl.ds(0, rows), :], heads[at], zero_sem.at[2 * at + 1])
+        blanks.append((me + distance >= devices, blank))
+
+    filter_copies = []
+    for offset in range(1, devices if gather else 1):
+        peer = lax.rem(me + offset, devices)
+        filter_copies.append(
+            axis_copy(packed, mine, filter_send.at[offset], filter_recv.at[offset], "ctx", peer)
+        )
+
+    for missing, blank in blanks:
+        pl.when(missing)(blank.start)
+    greet(("ctx",))
+    for distance, copy in head_copies:
+        pl.when(me >= distance)(copy.start)
+    live = count[0, 0]
+    col = lax.broadcasted_iota(jnp.int32, (widest, cap), 1)
+    row = lax.broadcasted_iota(jnp.int32, (widest, cap), 0)
+    pick = jnp.where(col - row == live - widest, 1.0, 0.0).astype(BF16)
+    width = min(512, channels)
+    for start in range(0, channels, width):
+        span = slice(start, start + width)
+        last[:widest, span] = dot(pick, kept[1, 0, :, span]).astype(BF16)
+        last[widest : 2 * widest, span] = dot(pick, kept[2, 0, :, span]).astype(BF16)
+        last[2 * widest :, span] = dot(pick[widest - 16 :], kept[0, 0, :, span]).astype(BF16)
+    for distance, copy in tail_copies:
+        pl.when(me + distance < devices)(copy.start)
+    for copy in filter_copies:
+        copy.start()
+    for missing, blank in blanks:
+        pl.when(missing)(blank.wait)
+    own.wait()
+    for distance, copy in head_copies:
+        pl.when(me >= distance)(copy.wait_send)
+        pl.when(me + distance < devices)(copy.wait_recv)
+    for distance, copy in tail_copies:
+        pl.when(me + distance < devices)(copy.wait_send)
+        pl.when(me >= distance)(copy.wait_recv)
+    for copy in filter_copies:
+        copy.wait_send()
+        copy.wait_recv()
+
+
+def exchange(plan, devices, streams, cotangent, counts, packed):
+    channels = streams.shape[3]
+    width = packed.shape[1] * (devices if packed.shape[1] % 128 == 0 else 1)
+    tails = [2 * big + small for big, small in plan]
+    heads = [2 * big + 2 * small for big, small in plan]
+    copies = 8 * len(plan)
+    out = pl.pallas_call(
+        functools.partial(exchange_kernel, plan, devices),
+        in_specs=[
+            pl.BlockSpec(memory_space=pltpu.SMEM),
+            pl.BlockSpec(memory_space=pltpu.VMEM),
+        ]
+        + [pl.BlockSpec(memory_space=pl.ANY)] * 3,
+        out_specs=[pl.BlockSpec(memory_space=pl.ANY)] * (2 * len(plan) + 1),
+        out_shape=[jax.ShapeDtypeStruct((rows, channels), BF16) for rows in tails + heads]
+        + [jax.ShapeDtypeStruct((packed.shape[0], width), BF16)],
+        scratch_shapes=[
+            pltpu.VMEM((2 * plan[0][0] + 16, channels), BF16),
+            pltpu.VMEM((max(heads), channels), BF16),
+            pltpu.SemaphoreType.DMA((copies,)),
+            pltpu.SemaphoreType.DMA((copies,)),
+            pltpu.SemaphoreType.DMA((devices,)),
+            pltpu.SemaphoreType.DMA((devices,)),
+            pltpu.SemaphoreType.DMA,
+            pltpu.SemaphoreType.DMA((2 * len(plan),)),
+        ],
+        compiler_params=pltpu.CompilerParams(
+            collective_id=0, has_side_effects=True, vmem_limit_bytes=32 * 1024 * 1024
+        ),
+        name="exchange",
+    )(counts, streams, streams, cotangent, packed)
+    return out[: len(plan)], out[len(plan) : 2 * len(plan)], out[2 * len(plan)]
+
+
+def reduce_kernel(
+    devices, groups, sums, long_out, short_out,
+    outgoing, incoming, total, dp_parts, ctx_parts, send, recv, dp_send, dp_recv, ctx_send, ctx_recv,
+):
+    me = lax.axis_index("ctx")
+    group = lax.axis_index("dp")
+    share = long_out.shape[1]
+
+    def columns(device):
+        return pl.ds(pl.multiple_of(device * share, share), share)
+
+    greet(("ctx", "dp"))
+    copies = []
+    for offset in range(1, devices):
+        peer = lax.rem(me + offset, devices)
+        outgoing[offset] = sums[:, columns(peer)].astype(BF16)
+        copy = axis_copy(
+            outgoing.at[offset], incoming.at[offset], send.at[offset], recv.at[offset], "ctx", peer
+        )
+        copy.start()
+        copies.append(copy)
+    total[...] = sums[:, columns(me)]
+    for offset in range(1, devices):
+        copies[offset - 1].wait_recv()
+        total[...] += incoming[offset].astype(F32)
+    squares = jnp.zeros((8, 128), F32)
+    for row in range(0, GROWS, 8):
+        for col in range(0, share, 128):
+            part = total[row : row + 8, col : col + 128]
+            squares = squares + part * part
+    for axis, size, mine, parts, out_sem, in_sem in (
+        ("dp", groups, group, dp_parts, dp_send, dp_recv),
+        ("ctx", devices, me, ctx_parts, ctx_send, ctx_recv),
+    ):
+        parts[0] = squares
+        for offset in range(1, size):
+            copy = axis_copy(
+                parts.at[0], parts.at[offset], out_sem.at[offset], in_sem.at[offset],
+                axis, lax.rem(mine + offset, size),
+            )
+            copy.start()
+            copies.append(copy)
+        for offset in range(1, size):
+            copies[offset - size].wait_recv()
+            squares = squares + parts[offset]
+    for copy in copies:
+        copy.wait_send()
+    whole = jnp.sum(jnp.sum(squares, axis=0, keepdims=True), axis=1, keepdims=True)
+    rms = jnp.sqrt(whole / float((LTAP + 3 * STAP) * CH) + 1e-06)
+    long_out[...] = total[:LTAP, :] / rms
+    short_out[...] = total[LTAP:, :] / rms
+
+
+def reduce_sums(sums, devices, groups):
+    share = sums.shape[1] // devices
+    dma = pltpu.SemaphoreType.DMA
+    return pl.pallas_call(
+        functools.partial(reduce_kernel, devices, groups),
+        in_specs=[pl.BlockSpec(memory_space=pltpu.VMEM)],
+        out_specs=[pl.BlockSpec(memory_space=pltpu.VMEM)] * 2,
+        out_shape=[
+            jax.ShapeDtypeStruct((LTAP, share), F32),
+            jax.ShapeDtypeStruct((GROWS - LTAP, share), F32),
+        ],
+        scratch_shapes=[
+            pltpu.VMEM((devices, GROWS, share), BF16),
+            pltpu.VMEM((devices, GROWS, share), BF16),
+            pltpu.VMEM((GROWS, share), F32),
+            pltpu.VMEM((groups, 8, 128), F32),
+            pltpu.VMEM((devices, 8, 128), F32),
+            dma((devices,)),
+            dma((devices,)),
+            dma((groups,)),
+            dma((groups,)),
+            dma((devices,)),
+            dma((devices,)),
+        ],
+        compiler_params=pltpu.CompilerParams(
+            collective_id=1, has_side_effects=True, vmem_limit_bytes=32 * 1024 * 1024
+        ),
+        name="reduce_sums",
+    )(sums)
 
 
 def halo_info(counts, me, plan):
-    devices = counts.shape[0]
-    ids = jnp.arange(devices, dtype=jnp.int32)
-
-    def total(first, end):
-        return jnp.sum(jnp.where((ids >= first) & (ids < end), counts, 0))
-
-    numbers = [total(me, me + 1), total(me, devices)]
+    ids = jnp.arange(counts.shape[0], dtype=jnp.int32)
+    spans = [(0, 1), (0, counts.shape[0])]
     for distance in range(1, len(plan) + 1):
-        numbers += [
-            total(me - distance + 1, me),
-            total(me - distance, me - distance + 1),
-            total(me, me + distance),
-            total(me + distance, me + distance + 1),
-        ]
-    return jnp.stack(numbers).astype(jnp.int32)
+        spans += [(1 - distance, 0), (-distance, 1 - distance), (0, distance), (distance, distance + 1)]
+    spans = np.asarray(spans, np.int32)
+    at = ids[None, :] - me
+    inside = (at >= spans[:, :1]) & (at < spans[:, 1:])
+    return jnp.sum(jnp.where(inside, counts[None, :], 0), axis=1)
 
 
 def local(streams, cotangent, counts, short_filters, long_filter):
     devices = lax.axis_size("ctx")
     me = lax.axis_index("ctx")
     live_count = counts[0, 0]
-    cap = streams.shape[2]
     share = long_filter.shape[1]
-    plan = halo_plan(devices, cap)
-    q0, k0, v0 = streams[0, 0], streams[1, 0], streams[2, 0]
-    dy = cotangent[0]
+    plan = halo_plan(devices, streams.shape[2])
     digits = jnp.stack([live_count // 16, live_count % 16]).astype(BF16)
     packed = jnp.concatenate(
         [
@@ -327,30 +552,20 @@
         ],
         axis=0,
     )
-    filters = lax.all_gather(packed, "ctx", axis=1, tiled=True)
+    tails, heads, filters = exchange(plan, devices, streams, cotangent, counts, packed)
+    if share % 128:
+        filters = lax.all_gather(packed, "ctx", axis=1, tiled=True)
     digits = filters[LTAP + 3 * STAP : LTAP + 3 * STAP + 2, ::share].astype(jnp.int32)
     info = halo_info(digits[0] * 16 + digits[1], me, plan)
-    widest = plan[0][0]
-    tail = last_rows(streams[:, 0], live_count, widest)
-    tails, heads = [], []
-    for at, (big, small) in enumerate(plan):
-        distance = at + 1
-        later = [(j, j + distance) for j in range(devices - distance)]
-        earlier = [(j + distance, j) for j in range(devices - distance)]
-        last = [tail[1, widest - big :], tail[2, widest - big :]]
-        first = [q0[:big], dy[:big]]
-        if small:
-            last.append(tail[0, widest - small :])
-            first += [k0[:small], v0[:small]]
-        tails.append(lax.ppermute(jnp.concatenate(last, axis=0), "ctx", later))
-        heads.append(lax.ppermute(jnp.concatenate(first, axis=0), "ctx", earlier))
     stream_grads, sums = run_blocks(plan, info, tails, heads, streams, cotangent, filters)
-    own = lax.psum_scatter(sums, "ctx", scatter_dimension=1, tiled=True)
-    squares = lax.psum(jnp.sum(own * own), ("dp", "ctx"))
-    rms = jnp.sqrt(squares / float((LTAP + 3 * STAP) * CH) + 1e-06)
-    normed = own / rms
-    long_grad = normed[:LTAP]
-    short_grad = normed[LTAP : LTAP + 3 * STAP].reshape(3, STAP, share)
+    if share % 128:
+        own = lax.psum_scatter(sums, "ctx", scatter_dimension=1, tiled=True)
+        squares = lax.psum(jnp.sum(own * own), ("dp", "ctx"))
+        own = own / jnp.sqrt(squares / float((LTAP + 3 * STAP) * CH) + 1e-06)
+        long_grad, short_rows = own[:LTAP], own[LTAP:]
+    else:
+        long_grad, short_rows = reduce_sums(sums, devices, lax.axis_size("dp"))
+    short_grad = short_rows[: 3 * STAP].reshape(3, STAP, share)
     return (stream_grads, long_grad, short_grad)
 
 

time: 263 us -> 183 us (0.70)
  Pallas kernels: 44.9 us -> 162 us
  blocking collectives: 108 us -> 0 us
  waiting for transfers between devices: 52.4 us -> 0 us
  starting transfers between devices: 16.8 us -> 0 us
  between operations: 15.7 us -> 1.41 us
  other arithmetic: 6.6 us -> 1.13 us
    pallas_call x0 -> x2, Pallas kernels: none -> 117 us  [the longest x1 97.6 us: exchange(): pl.pallas_call(functools.partial(exchange_kernel, plan, devices), in_spec...]
    all_gather x1 -> x0, blocking collectives: 68.8 us -> none  [local(): filters = lax.all_gather(packed, 'ctx', axis=1, tiled=True)]
    psum x1 -> x0, blocking collectives: 39.5 us -> none  [local(): squares = lax.psum(jnp.sum(own * own), ('dp', 'ctx'))]
    reduce_scatter x1 -> x0, waiting for transfers between devices: 36.7 us -> none  [local(): own = lax.psum_scatter(sums, 'ctx', scatter_dimension=1, tiled=True)]
    ppermute x6 -> x0, starting transfers between devices: 16.7 us -> none  [the longest x3 12.9 us: local(): tails.append(lax.ppermute(jnp.concatenate(last, axis=0), 'ctx', later))]
    ppermute x6 -> x0, waiting for transfers between devices: 15.8 us -> none  [the longest x3 15.7 us: local(): tails.append(lax.ppermute(jnp.concatenate(last, axis=0), 'ctx', later))]
    unnamed x18 -> x35, local copies, waits for them, and re-layouts: 3.65 us -> 15.8 us
    another operation x1 -> x0, local copies, waits for them, and re-layouts: 8.83 us -> none  [halo_info(): return jnp.stack(numbers).astype(jnp.int32)]
  transfers between devices with their start and end apart: 7 -> 0, of which waited for: 2 -> 0; matrix products, arithmetic and copies ran while one was open for 5% -> 0% of each run, Pallas kernels for 0% -> 0%
where the time goes in v2:
time: 183 us; the launch traced here: 182 us
  Pallas kernels  162 us (89%)
  local copies, waits for them, and re-layouts  17.3 us (9%)
    pallas_call x1, Pallas kernels, exchange(): pl.pallas_call(functools.partial(exchange_kernel, plan, devices), in_spec...  97.6 us
    pallas_call x1, Pallas kernels, run_blocks(): pl.pallas_call(functools.partial(block_kernel, plan, cap), grid=(channels...  45.7 us
    pallas_call x1, Pallas kernels, reduce_sums(): pl.pallas_call(functools.partial(reduce_kernel, devices, groups), in_spec...  18.9 us
    unnamed x35, local copies, waits for them, and re-layouts  15.8 us

profile of v2, /device:TPU:0, one launch (start us, length us, event | category | flops | bytes accessed | tf_op | source)
XLA Modules:
  0.0 182.0 jit_solution(11165159783825462812)
XLA Ops:
  1.3 0.1 pad_maximum_fusion
  1.4 0.1 pad.3.clone
  1.5 0.7 reshape.36
  2.2 0.9 maximum_maximum_fusion.packed
  3.2 0.0 copy-start
  3.2 2.1 %copy-done = bf16[3,1,320,2048]{3,2,1,0:T(8,128)(2,1)S(1)} copy-done((bf16[3,1,320,2048]{3,2,1,0:T(8,128)(2,1)S(1)}, bf16[3,1,320,2048]{3,2,1,0:T(8,128)(2,1)}, u32[]{:S(2)}) %copy-start) | copy-done | bytes 3932184
  5.3 0.0 copy-start.1
  5.3 1.3 copy-done.1
  6.6 0.0 copy-start.15
  6.6 97.6 %exchange.1 = (bf16[304,2048]{1,0:T(8,128)(2,1)S(1)}, bf16[304,2048]{1,0:T(8,128)(2,1)S(1)}, bf16[32,2048]{1,0:T(8,128)(2,1)S(1)}, bf16[320,2048]{1,0:T(8,128)(2...) custom-call(s32[1,1]{1,0:T(1,128)} %copy.17.count, ...), custom_call_target="tpu_custom_call" | custom-call | tf_op jit(solution)/shard_map/exchange/pallas_call | solution.py:416
  104.2 0.0 copy-start.3
  104.2 1.1 copy-done.3
  105.3 1.1 copy-done.4
  106.4 0.7 copy-done.11
  107.0 0.7 copy-done.13
  107.7 0.1 slice.12
  107.8 0.0 copy-done.15
  107.8 0.0 copy-done.16
  107.8 0.1 select_reduce_fusion.info
  107.9 0.0 copy-done.9
  107.9 1.0 copy-done.5
  108.9 1.0 copy-done.6
  109.9 1.0 copy-done.7
  111.0 1.0 copy-done.8
  112.0 1.0 copy-done.10
  113.0 0.9 copy-done.12
  113.9 0.9 copy-done.14
  114.8 45.7 %hyena_blocks.1 = (bf16[3,1,320,2048]{3,2,1,0:T(8,128)(2,1)}, f32[160,2048]{1,0:T(8,128)}) custom-call(s32[14]{0:T(128)S(1)} %select_reduce_fusion.info, bf16[304,2048]{1,0:T(8,128)(2,1)S(1)} %get-tuple-element.15.refs_0_, bf16[304,2048]{1,0:T(8,128)(2,1)S(1)} %get-tuple-element.16.refs_1_, bf16[32,2048]{1,0:T(8,128)(2,1)S(1)} %copy-done.12, ...), custom_call_target="tpu_custom_call" | custom-call | tf_op jit(solution)/shard_map/hyena_blocks/pallas_call | solution.py:262
  160.5 1.3 copy-done.2
  161.8 18.9 %reduce_sums.1 = (f32[128,256]{1,0:T(8,128)S(1)}, f32[32,256]{1,0:T(8,128)S(1)}) custom-call(f32[160,2048]{1,0:T(8,128)S(1)} %copy-done.2), custom_call_target="tpu_custom_call" | custom-call | tf_op jit(solution)/shard_map/reduce_sums/pallas_call | solution.py:500
  180.7 0.6 reshape.37
  181.3 0.7 copy.18
  (18 shorter events, 0.0 us)
Async XLA Ops:
  3.2 2.1 %copy-start = (bf16[3,1,320,2048]{3,2,1,0:T(8,128)(2,1)S(1)}, bf16[3,1,320,2048]{3,2,1,0:T(8,128)(2,1)}, u32[]{:S(2)}) copy-start(bf16[3,1,320,2048]{3,2,1,0:T(8,128)(2,1)} %refs_6_.1) | copy-start | bytes 11796484
  5.3 1.3 copy-start.1
  6.6 101.2 %copy-start.15 = (s32[14]{0:T(128)S(1)}, s32[14]{0:T(128)}, u32[]{:S(2)}) copy-start(s32[14]{0:T(128)} %constant.60) | copy-start | bytes 172
  6.6 101.2 %copy-start.16 = (s32[14]{0:T(128)S(1)}, s32[14]{0:T(128)}, u32[]{:S(2)}) copy-start(s32[14]{0:T(128)} %constant.59) | copy-start | bytes 172
  6.6 101.3 %copy-start.9 = (bf16[336,480]{1,0:T(8,128)(2,1)S(1)}, bf16[336,480]{1,0:T(8,128)(2,1)}, u32[]{:S(2)}) copy-start(bf16[336,480]{1,0:T(8,128)(2,1)} %constant.57.clone.refs_14_) | copy-start | bytes 967684
  104.2 1.1 copy-start.3
  105.3 1.1 copy-start.4
  106.4 0.7 copy-start.11
  107.0 0.7 copy-start.13
  107.9 1.0 copy-start.5
  108.9 1.0 copy-start.6
  109.9 1.0 copy-start.7
  111.0 1.0 copy-start.8
  112.0 1.0 copy-start.10
  113.0 0.9 copy-start.12
  113.9 0.9 copy-start.14
  160.5 1.3 copy-start.2

commit v3 on v2

--- a/solution.py
+++ b/solution.py
@@ -279,7 +279,7 @@
             jax.ShapeDtypeStruct((GROWS, channels), F32),
         ],
         scratch_shapes=scratch,
-        compiler_params=pltpu.CompilerParams(vmem_limit_bytes=48 * 1024 * 1024),
+        compiler_params=pltpu.CompilerParams(vmem_limit_bytes=60 * 1024 * 1024),
         name="hyena_blocks",
     )(info, *tails, *heads, streams, cotangent, filters, *[jnp.asarray(m) for m in matrices])
 
@@ -326,6 +326,10 @@
     own.start()
     zeros[...] = jnp.zeros_like(zeros)
 
+    relayed = len(plan) > 1 and plan[0] == plan[1]
+    even = lax.rem(me, 2) == 0
+    odd = lax.rem(me, 2) == 1
+    head_relays, tail_relays = [], []
     head_copies, tail_copies, blanks = [], [], []
     slot = 0
     for at, (big, small) in enumerate(plan):
@@ -346,6 +350,12 @@
             copy = axis_copy(source, target, send.at[slot], recv.at[slot], "ctx", before)
             head_copies.append((distance, copy))
             slot += 1
+            if relayed and at == 1:
+                passed = heads[0].at[pl.ds(first, rows), :]
+                head_relays.append(
+                    axis_copy(passed, target, send.at[slot], recv.at[slot - 1], "ctx", jnp.maximum(me - 1, 0))
+                )
+                slot += 1
         if big == widest and small:
             pieces = [(last, 0, 2 * widest + small)]
         else:
@@ -360,6 +370,14 @@
             copy = axis_copy(source, target, send.at[slot], recv.at[slot], "ctx", after)
             tail_copies.append((distance, copy))
             slot += 1
+            if relayed and at == 1:
+                passed = tails[0].at[pl.ds(first, rows), :]
+                tail_relays.append(
+                    axis_copy(
+                        passed, target, send.at[slot], recv.at[slot - 1], "ctx", jnp.minimum(me + 1, devices - 1)
+                    )
+                )
+                slot += 1
         rows = tails[at].shape[0]
         blank = pltpu.make_async_copy(zeros.at[pl.ds(0, rows), :], tails[at], zero_sem.at[2 * at])
         blanks.append((me < distance, blank))
@@ -377,8 +395,15 @@
     for missing, blank in blanks:
         pl.when(missing)(blank.start)
     greet(("ctx",))
+    def sends_head(distance):
+        return (me >= distance) & odd if relayed and distance == 2 else me >= distance
+
+    def sends_tail(distance):
+        fits = me + distance < devices
+        return fits & even if relayed and distance == 2 else fits
+
     for distance, copy in head_copies:
-        pl.when(me >= distance)(copy.start)
+        pl.when(sends_head(distance))(copy.start)
     live = count[0, 0]
     col = lax.broadcasted_iota(jnp.int32, (widest, cap), 1)
     row = lax.broadcasted_iota(jnp.int32, (widest, cap), 0)
@@ -390,18 +415,36 @@
         last[widest : 2 * widest, span] = dot(pick, kept[2, 0, :, span]).astype(BF16)
         last[2 * widest :, span] = dot(pick[widest - 16 :], kept[0, 0, :, span]).astype(BF16)
     for distance, copy in tail_copies:
-        pl.when(me + distance < devices)(copy.start)
+        pl.when(sends_tail(distance))(copy.start)
     for copy in filter_copies:
         copy.start()
     for missing, blank in blanks:
         pl.when(missing)(blank.wait)
     own.wait()
+    pass_head = odd & (me + 1 < devices)
+    pass_tail = even & (me >= 1) & (me + 1 < devices)
     for distance, copy in head_copies:
-        pl.when(me >= distance)(copy.wait_send)
-        pl.when(me + distance < devices)(copy.wait_recv)
+        if distance == 1:
+            pl.when(me + 1 < devices)(copy.wait_recv)
+    for copy in head_relays:
+        pl.when(pass_head)(copy.start)
     for distance, copy in tail_copies:
-        pl.when(me + distance < devices)(copy.wait_send)
-        pl.when(me >= distance)(copy.wait_recv)
+        if distance == 1:
+            pl.when(me >= 1)(copy.wait_recv)
+    for copy in tail_relays:
+        pl.when(pass_tail)(copy.start)
+    for distance, copy in head_copies:
+        pl.when(sends_head(distance))(copy.wait_send)
+        if distance > 1:
+            pl.when(me + distance < devices)(copy.wait_recv)
+    for distance, copy in tail_copies:
+        pl.when(sends_tail(distance))(copy.wait_send)
+        if distance > 1:
+            pl.when(me >= distance)(copy.wait_recv)
+    for copy in head_relays:
+        pl.when(pass_head)(copy.wait_send)
+    for copy in tail_relays:
+        pl.when(pass_tail)(copy.wait_send)
     for copy in filter_copies:
         copy.wait_send()
         copy.wait_recv()

time: 183 us -> 152 us (0.83)
  Pallas kernels: 162 us -> 136 us
  local copies, waits for them, and re-layouts: 17.3 us -> 12.6 us
    pallas_call x1, Pallas kernels: 97.6 us -> 69.8 us  [exchange(): pl.pallas_call(functools.partial(exchange_kernel, plan, devices), in_spec...]
    unnamed x35 -> x25, local copies, waits for them, and re-layouts: 15.8 us -> 11.1 us
where the time goes in v3:
time: 152 us; the launch traced here: 151 us
  Pallas kernels  136 us (89%)
  local copies, waits for them, and re-layouts  12.6 us (8%)
  other arithmetic  1.64 us (1%)
    pallas_call x1, Pallas kernels, exchange(): pl.pallas_call(functools.partial(exchange_kernel, plan, devices), in_spec...  69.8 us
    pallas_call x1, Pallas kernels, run_blocks(): pl.pallas_call(functools.partial(block_kernel, plan, cap), grid=(channels...  46.6 us
    pallas_call x1, Pallas kernels, reduce_sums(): pl.pallas_call(functools.partial(reduce_kernel, devices, groups), in_spec...  19.3 us
    unnamed x25, local copies, waits for them, and re-layouts  11.1 us

profile of v3, /device:TPU:0, one launch (start us, length us, event | category | flops | bytes accessed | tf_op | source)
XLA Modules:
  0.0 151.3 jit_solution(15095296269839156725)
XLA Ops:
  1.3 0.1 pad_maximum_fusion
  1.4 0.1 pad.3.clone
  1.5 0.7 reshape.36
  2.2 0.9 maximum_maximum_fusion.packed
  3.2 0.0 copy-start
  3.2 2.1 %copy-done = bf16[3,1,320,2048]{3,2,1,0:T(8,128)(2,1)S(1)} copy-done((bf16[3,1,320,2048]{3,2,1,0:T(8,128)(2,1)S(1)}, bf16[3,1,320,2048]{3,2,1,0:T(8,128)(2,1)}, u32[]{:S(2)}) %copy-start) | copy-done | bytes 3932184
  5.3 0.0 copy-start.1
  5.3 1.3 copy-done.1
  6.6 0.0 copy-start.10
  6.6 0.0 copy-start.11
  6.6 69.8 %exchange.1 = (bf16[304,2048]{1,0:T(8,128)(2,1)S(1)}, bf16[304,2048]{1,0:T(8,128)(2,1)S(1)}, bf16[32,2048]{1,0:T(8,128)(2,1)S(1)}, bf16[320,2048]{1,0:T(8,128)(2...) custom-call(s32[1,1]{1,0:T(1,128)} %copy.17.count, ...), custom_call_target="tpu_custom_call" | custom-call | tf_op jit(solution)/shard_map/exchange/pallas_call | solution.py:459
  76.4 0.0 copy-start.3
  76.4 1.1 copy-done.3
  77.5 0.0 copy-start.4
  77.5 1.1 copy-done.4
  78.6 0.0 copy-start.5
  78.6 1.0 copy-done.5
  79.6 0.0 copy-start.6
  79.6 1.1 copy-done.6
  80.7 0.7 copy-done.8
  81.3 0.7 copy-done.9
  82.0 0.1 slice.12
  82.1 0.0 copy-done.10
  82.1 0.0 copy-done.11
  82.1 0.6 select_reduce_fusion.info
  82.7 0.1 copy-done.7
  82.8 46.6 %hyena_blocks.1 = (bf16[3,1,320,2048]{3,2,1,0:T(8,128)(2,1)}, f32[160,2048]{1,0:T(8,128)}) custom-call(s32[14]{0:T(128)} %select_reduce_fusion.info, bf16[304,2048]{1,0:T(8,128)(2,1)} %copy-done.5, bf16[304,2048]{1,0:T(8,128)(2,1)} %copy-done.6, bf16[32,2048]{1,0:T(8,128)(2,1)} %copy-done.8, bf16[320,2048]{1,0:T(8,128)(2,1)} %copy-done.3, ...), custom_call_target="tpu_custom_call" | custom-call | tf_op jit(solution)/shard_map/hyena_blocks/pallas_call | solution.py:262
  129.4 0.0 copy-start.2
  129.4 1.3 copy-done.2
  130.7 19.3 %reduce_sums.1 = (f32[128,256]{1,0:T(8,128)S(1)}, f32[32,256]{1,0:T(8,128)S(1)}) custom-call(f32[160,2048]{1,0:T(8,128)S(1)} %copy-done.2), custom_call_target="tpu_custom_call" | custom-call | tf_op jit(solution)/shard_map/reduce_sums/pallas_call | solution.py:543
  150.1 0.6 reshape.37
  150.7 0.7 copy.18
  (8 shorter events, 0.0 us)
Async XLA Ops:
  3.2 2.1 %copy-start = (bf16[3,1,320,2048]{3,2,1,0:T(8,128)(2,1)S(1)}, bf16[3,1,320,2048]{3,2,1,0:T(8,128)(2,1)}, u32[]{:S(2)}) copy-start(bf16[3,1,320,2048]{3,2,1,0:T(8,128)(2,1)} %refs_6_.1) | copy-start | bytes 11796484
  5.3 1.3 copy-start.1
  6.6 75.5 %copy-start.10 = (s32[14]{0:T(128)S(1)}, s32[14]{0:T(128)}, u32[]{:S(2)}) copy-start(s32[14]{0:T(128)} %constant.60) | copy-start | bytes 172
  6.6 75.5 %copy-start.11 = (s32[14]{0:T(128)S(1)}, s32[14]{0:T(128)}, u32[]{:S(2)}) copy-start(s32[14]{0:T(128)} %constant.59) | copy-start | bytes 172
  76.4 1.1 copy-start.3
  77.5 1.1 copy-start.4
  78.6 1.0 copy-start.5
  79.6 1.1 copy-start.6
  80.7 0.7 copy-start.8
  81.3 0.7 copy-start.9
  82.0 0.9 copy-start.7
  129.4 1.3 copy-start.2
